TPU v7x, 32 devices: a whole 2x2x4 slice. The times are simulated.
32 devices in a mesh: groups: 2 (over y), ctx: 4 (over z), head: 2 (over x), sub: 2 (over core).
Axes of the slice: x: 2, y: 2, z: 4, core: 2. Of those that a mesh axis runs over, the one named last changes fastest.
Arguments:
- query_rows: bfloat16 [128, 128, 1024], P(('groups', 'ctx', 'sub'), 'head'), parts along dimension 0, may hold values from -16 to 16
- key_rows: bfloat16 [128, 128, 1024], P(('groups', 'ctx', 'sub'), 'head'), parts along dimension 0, may hold values from -6 to 6
- value_rows: bfloat16 [128, 128, 1024], P(('groups', 'ctx', 'sub'), 'head'), parts along dimension 0, may hold values from -4 to 4
- cotangent: bfloat16 [128, 128, 1024], P(('groups', 'ctx', 'sub'), 'head'), parts along dimension 0, may hold values from -4 to 4
- neighbours: int32 [128, 16], P('groups'), parts along dimension 0, may hold values from -1 to 63, as said below
- valid_counts: int32 [128], P('groups'), parts along dimension 0, may hold values from 32 to 128
Outputs:
- attended: bfloat16 [128, 128, 1024], P(('groups', 'ctx', 'sub'), 'head'), parts along dimension 0
- query_grad: bfloat16 [128, 128, 1024], P(('groups', 'ctx', 'sub'), 'head'), parts along dimension 0
- key_grad: bfloat16 [128, 128, 1024], P(('groups', 'ctx', 'sub'), 'head'), parts along dimension 0
- value_grad: bfloat16 [128, 128, 1024], P(('groups', 'ctx', 'sub'), 'head'), parts along dimension 0
There are 2 independent parts, one for each index of `groups`. A program takes and returns all parts, laid end to end along the dimension named above; each array names one. Nothing has to cross between parts.
Inputs may be any that keep to these rules, and one draw needn't show every extreme that they name: `neighbours`: row b begins with b itself; its other entries are distinct blocks at most 8 blocks away from b, or -1 for an empty slot; a block with 8 blocks on both sides has no empty slot.
All inputs are finite; a program needn't handle non-finite values.
Results may differ from a plain program's by a relative error of at most 0.012.
Values may be sent and summed in bfloat16 or wider, within the bound.
A program may use at most 128 MiB of HBM per device.

v0:
```python
import jax
import jax.numpy as jnp
from jax import lax
from jax.sharding import PartitionSpec as P

DH = 128
BQ = 128


NEGATIVE = -1e30


def from_behind(array, axis, by):
    devices = lax.axis_size(axis)
    pairs = [(i, i + by) for i in range(devices) if 0 <= i + by < devices]
    return lax.ppermute(array, axis, pairs)


def split_heads(tile_rows):
    return tile_rows.reshape(tile_rows.shape[0], tile_rows.shape[1] // DH, DH)


def lookup(count_table, wanted):
    matches = wanted[..., None] == jnp.arange(count_table.shape[0], dtype=jnp.int32)
    return jnp.sum(jnp.where(matches, count_table, 0), axis=-1)


def key_mask(block_lists, count_table):
    key_count = jnp.where(block_lists >= 0, lookup(count_table, block_lists), 0)
    positions = jnp.arange(BQ, dtype=jnp.int32)
    return (positions[None, None, :] < key_count[..., None]).reshape(block_lists.shape[0], -1)


def scores(query_block, key_block, usable_block):
    raw_scores = jnp.einsum(
        "qhd,khd->hqk",
        split_heads(query_block),
        split_heads(key_block),
        preferred_element_type=jnp.float32,
    )
    return jnp.where(usable_block[None, None, :], raw_scores * DH ** (-0.5), NEGATIVE)


def attend(query_block, key_block, value_block, usable_block, rows_ok):
    logits = scores(query_block, key_block, usable_block)
    highest = jnp.max(logits, axis=-1, keepdims=True)
    log_total = highest[..., 0] + jnp.log(jnp.sum(jnp.exp(logits - highest), axis=-1))
    probability = jnp.exp(logits - log_total[..., None]).astype(jnp.bfloat16)
    mixture = jnp.einsum(
        "hqk,khd->qhd", probability, split_heads(value_block), preferred_element_type=jnp.float32
    )
    mixture = jnp.where(rows_ok[:, None, None], mixture, 0.0)
    return (mixture.reshape(query_block.shape).astype(jnp.bfloat16), log_total)


def key_terms(
    query_block, key_block, value_block, grad_block, log_block, delta_block, usable_block
):
    probability = jnp.exp(scores(query_block, key_block, usable_block) - log_block[..., None])
    prob_grad = jnp.einsum(
        "qhd,khd->hqk",
        split_heads(grad_block),
        split_heads(value_block),
        preferred_element_type=jnp.float32,
    )
    score_grad = (probability * (prob_grad - delta_block[..., None])).astype(jnp.bfloat16)
    key_part = jnp.einsum(
        "hqk,qhd->khd", score_grad, split_heads(query_block), preferred_element_type=jnp.float32
    ) * DH ** (-0.5)
    value_part = jnp.einsum(
        "hqk,qhd->khd",
        probability.astype(jnp.bfloat16),
        split_heads(grad_block),
        preferred_element_type=jnp.float32,
    )
    return (score_grad, key_part.reshape(key_block.shape), value_part.reshape(key_block.shape))


def shards(query_rows, key_rows, value_rows, cotangent, neighbours, valid_counts):
    query_here, key_here, value_here, grad_here = (
        lax.all_to_all(query_rows, "head", split_axis=2, concat_axis=1, tiled=True),
        lax.all_to_all(key_rows, "head", split_axis=2, concat_axis=1, tiled=True),
        lax.all_to_all(value_rows, "head", split_axis=2, concat_axis=1, tiled=True),
        lax.all_to_all(cotangent, "head", split_axis=2, concat_axis=1, tiled=True),
    )
    blocks = query_here.shape[0]
    feature_width = query_here.shape[2]
    first_block = lax.axis_index(("ctx", "sub")) * blocks
    key_left, value_left = from_behind((key_here, value_here), ("ctx", "sub"), 1)
    key_right, value_right = from_behind((key_here, value_here), ("ctx", "sub"), -1)
    key_wide = jnp.concatenate([key_left, key_here, key_right], axis=0)
    value_wide = jnp.concatenate([value_left, value_here, value_right], axis=0)
    own_lists = lax.dynamic_slice_in_dim(neighbours, first_block, blocks, 0)
    own_counts = lax.dynamic_slice_in_dim(valid_counts, first_block, blocks, 0)
    positions = jnp.arange(BQ, dtype=jnp.int32)
    valid_rows = positions[None, :] < own_counts[:, None]
    slot_index = jnp.clip(own_lists - (first_block - blocks), 0, 3 * blocks - 1)
    usable = key_mask(own_lists, valid_counts)

    def forward_block(inputs):
        query_block, slot_block, usable_block, rows_ok = inputs
        key_block = key_wide[slot_block].reshape(-1, feature_width)
        value_block = value_wide[slot_block].reshape(-1, feature_width)
        return attend(query_block, key_block, value_block, usable_block, rows_ok)

    attended, log_total = lax.map(forward_block, (query_here, slot_index, usable, valid_rows))
    attended_out = lax.all_to_all(attended, "head", split_axis=1, concat_axis=2, tiled=True)
    grad_masked = jnp.where(valid_rows[:, :, None], grad_here, jnp.zeros_like(grad_here))
    heads_here = feature_width // DH
    row_delta = jnp.einsum(
        "bqhd,bqhd->bhq",
        grad_masked.reshape(blocks, BQ, heads_here, DH),
        attended.reshape(blocks, BQ, heads_here, DH),
        preferred_element_type=jnp.float32,
    )

    def own_block(running, inputs):
        key_sum, value_sum = running
        query_block, grad_block, log_block, delta_block, slot_block, usable_block = inputs
        key_block = key_wide[slot_block].reshape(-1, feature_width)
        value_block = value_wide[slot_block].reshape(-1, feature_width)
        score_grad, key_part, value_part = key_terms(
            query_block, key_block, value_block, grad_block, log_block, delta_block, usable_block
        )
        query_part = jnp.einsum(
            "hqk,khd->qhd", score_grad, split_heads(key_block), preferred_element_type=jnp.float32
        ) * DH ** (-0.5)
        key_sum = key_sum.at[slot_block].add(key_part.reshape(-1, BQ, feature_width))
        value_sum = value_sum.at[slot_block].add(value_part.reshape(-1, BQ, feature_width))
        return ((key_sum, value_sum), query_part.reshape(query_block.shape).astype(jnp.bfloat16))

    zeros_wide = jnp.zeros((3 * blocks, BQ, feature_width), jnp.float32)
    (key_sum, value_sum), query_grad = lax.scan(
        own_block,
        (zeros_wide, zeros_wide),
        (query_here, grad_masked, log_total, row_delta, slot_index, usable),
    )
    from_right = (
        from_behind(key_sum[:blocks].astype(jnp.bfloat16), ("ctx", "sub"), -1).astype(jnp.float32),
        from_behind(value_sum[:blocks].astype(jnp.bfloat16), ("ctx", "sub"), -1).astype(
            jnp.float32
        ),
    )
    from_left = (
        from_behind(key_sum[2 * blocks :].astype(jnp.bfloat16), ("ctx", "sub"), 1).astype(
            jnp.float32
        ),
        from_behind(value_sum[2 * blocks :].astype(jnp.bfloat16), ("ctx", "sub"), 1).astype(
            jnp.float32
        ),
    )
    key_total = key_sum[blocks : 2 * blocks] + from_right[0] + from_left[0]
    value_total = value_sum[blocks : 2 * blocks] + from_right[1] + from_left[1]
    key_grad = key_total.astype(jnp.bfloat16)
    value_grad = value_total.astype(jnp.bfloat16)
    query_out, key_out, value_out = (
        lax.all_to_all(query_grad, "head", split_axis=1, concat_axis=2, tiled=True),
        lax.all_to_all(key_grad, "head", split_axis=1, concat_axis=2, tiled=True),
        lax.all_to_all(value_grad, "head", split_axis=1, concat_axis=2, tiled=True),
    )
    return (attended_out, query_out, key_out, value_out)


def solution(mesh):
    placed = (
        P(("groups", "ctx", "sub"), "head", None),
        P(("groups", "ctx", "sub"), "head", None),
        P(("groups", "ctx", "sub"), "head", None),
        P(("groups", "ctx", "sub"), "head", None),
        P("groups", None),
        P("groups"),
    )
    return jax.shard_map(
        shards,
        mesh=mesh,
        in_specs=placed,
        out_specs=(
            P(("groups", "ctx", "sub"), "head", None),
            P(("groups", "ctx", "sub"), "head", None),
            P(("groups", "ctx", "sub"), "head", None),
            P(("groups", "ctx", "sub"), "head", None),
        ),
        check_vma=False,
    )
```

profile of v0, /device:TPU:0, one launch (start us, length us, event | category | flops | bytes accessed | tf_op | source)
XLA Modules:
  0.0 829.4 jit_solution(4601065322046602235)
XLA Ops:
  15.2 9.3 %all-to-all-done.2 = bf16[2,2,131072]{2,1,0:T(2,128)(2,1)S(1)} async-done(((bf16[2,2,131072]{2,1,0:T(2,128)(2,1)}), bf16[2,2,131072]{2,1,0:T(2,128)(2,1)S(1)}, u32[]{:S(2)}, u32[]{:S(2)}) %all-to-all-start.2) | async-done | bytes 1048608 | tf_op jit(solution)/shard_map/all_to_all | solution.py:82
  24.5 4.4 all-to-all-start
  34.1 8.2 all-to-all-done
  42.3 4.4 all-to-all-start.1
  83.8 6.5 all-to-all-done.4
  95.0 4.5 bitcast_convert_fusion
  109.3 159.6 %while.26 = (s32[]{:T(128)}, bf16[8,128,512]{1,2,0:T(8,128)(2,1)S(1)}, f32[8,4,128]{2,1,0:T(4,128)S(1)}, pred[8,128]{1,0:T(8,128)(4,1)S(1)}, s32[8,16]{1,0:T(8,1...) while((s32[]{:T(128)}, ...), condition=%wide.region_4.5_spmd, body=%wide.region_1.4_spmd.sunk | while | flops 544342592 | bytes 34368324 | solution.py:106
  279.2 456.6 %while.27 = (s32[]{:T(128)}, f32[24,128,512]{2,1,0:T(8,128)}, f32[24,128,512]{2,1,0:T(8,128)}, bf16[8,128,512]{1,2,0:T(8,128)(2,1)}, s32[8,16]{1,0:T(8,128)S(1)}...) while((s32[]{:T(128)}, f32[24,128,512]{2,1,0:T(8,128)}, ...), condition=%wide.region_8.9_spmd, body=%wide.region_5.8_spmd.sunk | while | flops 1352795136 | bytes 140139184 | solution.py:133
  302.5 5.3 copy.233
  312.1 5.3 copy.231
  317.3 9.3 %scatter_fusion = f32[24,128,512]{2,1,0:T(8,128)} fusion(f32[24,128,512]{2,1,0:T(8,128)} %get-tuple-element.443, s32[16]{0:T(128)S(1)} %fusion.67, f32[16,128,512]{2,1,0:T(8,128)} %copy.231), kind=kCustom, calls=%fused_computation.4.clone.1 | custom fusion | flops 1048576 | bytes 12582976 | tf_op jit(solution)/shard_map/while/body/eval_jaxpr/scatter-add | solution.py:128
  326.6 9.4 %scatter_fusion.1 = f32[24,128,512]{2,1,0:T(8,128)} fusion(f32[24,128,512]{2,1,0:T(8,128)} %get-tuple-element.444, s32[16]{0:T(128)S(1)} %fusion.67, f32[16,128,512]{2,1,0:T(8,128)} %copy.233), kind=kCustom, calls=%fused_computation.5.clone.1 | custom fusion | flops 1048576 | bytes 12582976 | tf_op jit(solution)/shard_map/while/body/eval_jaxpr/scatter-add | solution.py:129
  359.2 5.3 copy.233
  368.7 5.3 copy.231
  374.0 9.4 %scatter_fusion = f32[24,128,512]{2,1,0:T(8,128)} fusion(f32[24,128,512]{2,1,0:T(8,128)} %get-tuple-element.443, s32[16]{0:T(128)S(1)} %fusion.67, f32[16,128,512]{2,1,0:T(8,128)} %copy.231), kind=kCustom, calls=%fused_computation.4.clone.1 | custom fusion | flops 1048576 | bytes 12582976 | tf_op jit(solution)/shard_map/while/body/eval_jaxpr/scatter-add | solution.py:128
  383.3 9.5 %scatter_fusion.1 = f32[24,128,512]{2,1,0:T(8,128)} fusion(f32[24,128,512]{2,1,0:T(8,128)} %get-tuple-element.444, s32[16]{0:T(128)S(1)} %fusion.67, f32[16,128,512]{2,1,0:T(8,128)} %copy.233), kind=kCustom, calls=%fused_computation.5.clone.1 | custom fusion | flops 1048576 | bytes 12582976 | tf_op jit(solution)/shard_map/while/body/eval_jaxpr/scatter-add | solution.py:129
  415.9 5.3 copy.233
  425.5 5.3 copy.231
  430.8 9.4 %scatter_fusion = f32[24,128,512]{2,1,0:T(8,128)} fusion(f32[24,128,512]{2,1,0:T(8,128)} %get-tuple-element.443, s32[16]{0:T(128)S(1)} %fusion.67, f32[16,128,512]{2,1,0:T(8,128)} %copy.231), kind=kCustom, calls=%fused_computation.4.clone.1 | custom fusion | flops 1048576 | bytes 12582976 | tf_op jit(solution)/shard_map/while/body/eval_jaxpr/scatter-add | solution.py:128
  440.1 9.4 %scatter_fusion.1 = f32[24,128,512]{2,1,0:T(8,128)} fusion(f32[24,128,512]{2,1,0:T(8,128)} %get-tuple-element.444, s32[16]{0:T(128)S(1)} %fusion.67, f32[16,128,512]{2,1,0:T(8,128)} %copy.233), kind=kCustom, calls=%fused_computation.5.clone.1 | custom fusion | flops 1048576 | bytes 12582976 | tf_op jit(solution)/shard_map/while/body/eval_jaxpr/scatter-add | solution.py:129
  472.6 5.3 copy.233
  482.2 5.3 copy.231
  487.4 9.5 %scatter_fusion = f32[24,128,512]{2,1,0:T(8,128)} fusion(f32[24,128,512]{2,1,0:T(8,128)} %get-tuple-element.443, s32[16]{0:T(128)S(1)} %fusion.67, f32[16,128,512]{2,1,0:T(8,128)} %copy.231), kind=kCustom, calls=%fused_computation.4.clone.1 | custom fusion | flops 1048576 | bytes 12582976 | tf_op jit(solution)/shard_map/while/body/eval_jaxpr/scatter-add | solution.py:128
  497.0 9.5 %scatter_fusion.1 = f32[24,128,512]{2,1,0:T(8,128)} fusion(f32[24,128,512]{2,1,0:T(8,128)} %get-tuple-element.444, s32[16]{0:T(128)S(1)} %fusion.67, f32[16,128,512]{2,1,0:T(8,128)} %copy.233), kind=kCustom, calls=%fused_computation.5.clone.1 | custom fusion | flops 1048576 | bytes 12582976 | tf_op jit(solution)/shard_map/while/body/eval_jaxpr/scatter-add | solution.py:129
  529.7 5.3 copy.233
  539.2 5.3 copy.231
  544.5 9.6 %scatter_fusion = f32[24,128,512]{2,1,0:T(8,128)} fusion(f32[24,128,512]{2,1,0:T(8,128)} %get-tuple-element.443, s32[16]{0:T(128)S(1)} %fusion.67, f32[16,128,512]{2,1,0:T(8,128)} %copy.231), kind=kCustom, calls=%fused_computation.4.clone.1 | custom fusion | flops 1048576 | bytes 12582976 | tf_op jit(solution)/shard_map/while/body/eval_jaxpr/scatter-add | solution.py:128
  554.1 9.6 %scatter_fusion.1 = f32[24,128,512]{2,1,0:T(8,128)} fusion(f32[24,128,512]{2,1,0:T(8,128)} %get-tuple-element.444, s32[16]{0:T(128)S(1)} %fusion.67, f32[16,128,512]{2,1,0:T(8,128)} %copy.233), kind=kCustom, calls=%fused_computation.5.clone.1 | custom fusion | flops 1048576 | bytes 12582976 | tf_op jit(solution)/shard_map/while/body/eval_jaxpr/scatter-add | solution.py:129
  586.8 5.3 copy.233
  596.4 5.3 copy.231
  601.6 9.7 %scatter_fusion = f32[24,128,512]{2,1,0:T(8,128)} fusion(f32[24,128,512]{2,1,0:T(8,128)} %get-tuple-element.443, s32[16]{0:T(128)S(1)} %fusion.67, f32[16,128,512]{2,1,0:T(8,128)} %copy.231), kind=kCustom, calls=%fused_computation.4.clone.1 | custom fusion | flops 1048576 | bytes 12582976 | tf_op jit(solution)/shard_map/while/body/eval_jaxpr/scatter-add | solution.py:128
  611.3 9.6 %scatter_fusion.1 = f32[24,128,512]{2,1,0:T(8,128)} fusion(f32[24,128,512]{2,1,0:T(8,128)} %get-tuple-element.444, s32[16]{0:T(128)S(1)} %fusion.67, f32[16,128,512]{2,1,0:T(8,128)} %copy.233), kind=kCustom, calls=%fused_computation.5.clone.1 | custom fusion | flops 1048576 | bytes 12582976 | tf_op jit(solution)/shard_map/while/body/eval_jaxpr/scatter-add | solution.py:129
  644.0 5.3 copy.233
  653.6 5.3 copy.231
  658.9 9.8 %scatter_fusion = f32[24,128,512]{2,1,0:T(8,128)} fusion(f32[24,128,512]{2,1,0:T(8,128)} %get-tuple-element.443, s32[16]{0:T(128)S(1)} %fusion.67, f32[16,128,512]{2,1,0:T(8,128)} %copy.231), kind=kCustom, calls=%fused_computation.4.clone.1 | custom fusion | flops 1048576 | bytes 12582976 | tf_op jit(solution)/shard_map/while/body/eval_jaxpr/scatter-add | solution.py:128
  668.6 9.7 %scatter_fusion.1 = f32[24,128,512]{2,1,0:T(8,128)} fusion(f32[24,128,512]{2,1,0:T(8,128)} %get-tuple-element.444, s32[16]{0:T(128)S(1)} %fusion.67, f32[16,128,512]{2,1,0:T(8,128)} %copy.233), kind=kCustom, calls=%fused_computation.5.clone.1 | custom fusion | flops 1048576 | bytes 12582976 | tf_op jit(solution)/shard_map/while/body/eval_jaxpr/scatter-add | solution.py:129
  701.4 5.3 copy.233
  710.9 5.3 copy.231
  716.2 9.7 %scatter_fusion = f32[24,128,512]{2,1,0:T(8,128)} fusion(f32[24,128,512]{2,1,0:T(8,128)} %get-tuple-element.443, s32[16]{0:T(128)S(1)} %fusion.67, f32[16,128,512]{2,1,0:T(8,128)} %copy.231), kind=kCustom, calls=%fused_computation.4.clone.1 | custom fusion | flops 1048576 | bytes 12582976 | tf_op jit(solution)/shard_map/while/body/eval_jaxpr/scatter-add | solution.py:128
  725.9 9.7 %scatter_fusion.1 = f32[24,128,512]{2,1,0:T(8,128)} fusion(f32[24,128,512]{2,1,0:T(8,128)} %get-tuple-element.444, s32[16]{0:T(128)S(1)} %fusion.67, f32[16,128,512]{2,1,0:T(8,128)} %copy.233), kind=kCustom, calls=%fused_computation.5.clone.1 | custom fusion | flops 1048576 | bytes 12582976 | tf_op jit(solution)/shard_map/while/body/eval_jaxpr/scatter-add | solution.py:129
  735.8 6.1 copy.213
  744.7 6.3 collective-permute-start.5
  756.3 6.1 copy.212
  775.0 6.4 copy.177
  784.1 5.6 all-to-all-done.5
  793.3 6.4 copy.180
  802.7 4.5 all-to-all-done.6
  807.2 4.7 all-to-all-start.7
  (408 shorter events, 505.4 us)
Async XLA Ops:
  0.6 46.1 %copy-start = (s32[64,16]{0,1:T(8,128)S(1)}, s32[64,16]{0,1:T(8,128)}, u32[]{:S(2)}) copy-start(s32[64,16]{0,1:T(8,128)} %param.14) | copy-start | bytes 12292
  5.8 18.6 %all-to-all-start.2 = ((bf16[2,2,131072]{2,1,0:T(2,128)(2,1)}), bf16[2,2,131072]{2,1,0:T(2,128)(2,1)S(1)}, u32[]{:S(2)}, u32[]{:S(2)}) async-start(bf16[2,2,131072]{2,1,0:T(2,128)(2,1)} %reshape.242), calls=%async_computation.2 | async-start | bytes 2097152 | tf_op jit(solution)/shard_map/all_to_all | solution.py:82
  24.5 17.8 %all-to-all-start = ((bf16[2,2,131072]{2,1,0:T(2,128)(2,1)}), bf16[2,2,131072]{2,1,0:T(2,128)(2,1)}, u32[]{:S(2)}, u32[]{:S(2)}) async-start(bf16[2,2,131072]{2,1,0:T(2,128)(2,1)} %reshape.238), calls=%async_computation | async-start | bytes 2097152 | tf_op jit(solution)/shard_map/all_to_all | solution.py:83
  31.6 15.3 %copy-start.8 = (s32[64]{0:T(128)S(1)}, s32[64]{0:T(128)}, u32[]{:S(2)}) copy-start(s32[64]{0:T(128)} %param.15) | copy-start | bytes 772
  42.3 29.2 %all-to-all-start.1 = ((bf16[2,2,131072]{2,1,0:T(2,128)(2,1)}), bf16[2,2,131072]{2,1,0:T(2,128)(2,1)}, u32[]{:S(2)}, u32[]{:S(2)}) async-start(bf16[2,2,131072]{2,1,0:T(2,128)(2,1)} %reshape.240), calls=%async_computation.1 | async-start | bytes 2097152 | tf_op jit(solution)/shard_map/all_to_all | solution.py:81
  56.0 46.5 %collective-permute-start.3 = (bf16[8,128,512]{2,1,0:T(8,128)(2,1)}, bf16[8,128,512]{2,1,0:T(8,128)(2,1)}, u32[]{:S(2)}, u32[]{:S(2)}) collective-permute-start(bf16[8,128,512]{2,1,0:T(8,128)(2,1)} %bitcast.29), channel_id=1, source_target_pairs={{1,0},{4,1},{5,4},{8,5},{9,8},{12,9},{13,12},{3,2},{6,3},{7,6},{10... | collective-permute-start | bytes 3145736 | tf_op jit(solution)/shard_map/ppermute | solution.py:16
  57.3 45.3 %collective-permute-start.2 = (bf16[8,128,512]{2,1,0:T(8,128)(2,1)}, bf16[8,128,512]{2,1,0:T(8,128)(2,1)}, u32[]{:S(2)}, u32[]{:S(2)}) collective-permute-start(bf16[8,128,512]{2,1,0:T(8,128)(2,1)} %bitcast.29), channel_id=1, source_target_pairs={{0,1},{1,4},{4,5},{5,8},{8,9},{9,12},{12,13},{2,3},{3,6},{6,7},{7,... | collective-permute-start | bytes 3145736 | tf_op jit(solution)/shard_map/ppermute | solution.py:16
  66.2 39.6 %collective-permute-start.1 = (bf16[8,128,512]{2,1,0:T(8,128)(2,1)}, bf16[8,128,512]{2,1,0:T(8,128)(2,1)}, u32[]{:S(2)}, u32[]{:S(2)}) collective-permute-start(bf16[8,128,512]{2,1,0:T(8,128)(2,1)} %bitcast.21), channel_id=1, source_target_pairs={{1,0},{4,1},{5,4},{8,5},{9,8},{12,9},{13,12},{3,2},{6,3},{7,6},{10... | collective-permute-start | bytes 3145736 | tf_op jit(solution)/shard_map/ppermute | solution.py:16
  67.5 38.3 %collective-permute-start = (bf16[8,128,512]{2,1,0:T(8,128)(2,1)}, bf16[8,128,512]{2,1,0:T(8,128)(2,1)}, u32[]{:S(2)}, u32[]{:S(2)}) collective-permute-start(bf16[8,128,512]{2,1,0:T(8,128)(2,1)} %bitcast.21), channel_id=1, source_target_pairs={{0,1},{1,4},{4,5},{5,8},{8,9},{9,12},{12,13},{2,3},{3,6},{6,7},{7,... | collective-permute-start | bytes 3145736 | tf_op jit(solution)/shard_map/ppermute | solution.py:16
  71.6 18.8 %all-to-all-start.4 = ((bf16[2,2,131072]{2,1,0:T(2,128)(2,1)}), bf16[2,2,131072]{2,1,0:T(2,128)(2,1)S(1)}, u32[]{:S(2)}, u32[]{:S(2)}) async-start(bf16[2,2,131072]{2,1,0:T(2,128)(2,1)} %reshape.244), calls=%async_computation.4 | async-start | bytes 2097152 | tf_op jit(solution)/shard_map/all_to_all | solution.py:84
  268.9 6.9 copy-start.5
  293.8 1.3 copy-start.2
  295.1 1.6 copy-start.4
  296.6 1.6 copy-start.3
  350.4 1.3 copy-start.2
  351.7 1.6 copy-start.4
  353.3 1.6 copy-start.3
  407.2 1.3 copy-start.2
  408.5 1.6 copy-start.4
  410.1 1.6 copy-start.3
  463.9 1.3 copy-start.2
  465.2 1.6 copy-start.4
  466.8 1.6 copy-start.3
  520.9 1.3 copy-start.2
  522.2 1.6 copy-start.4
  523.8 1.6 copy-start.3
  578.1 1.3 copy-start.2
  579.4 1.6 copy-start.4
  580.9 1.6 copy-start.3
  635.3 1.3 copy-start.2
  636.6 1.6 copy-start.4
  638.2 1.6 copy-start.3
  692.6 1.3 copy-start.2
  693.9 1.6 copy-start.4
  695.5 1.6 copy-start.3
  742.0 9.0 %copy-start.6 = (bf16[8,128,512]{1,2,0:T(8,128)(2,1)S(1)}, bf16[8,128,512]{1,2,0:T(8,128)(2,1)}, u32[]{:S(2)}) copy-start(bf16[8,128,512]{1,2,0:T(8,128)(2,1)} %copy-done.5) | copy-start | bytes 3145732
  743.4 38.0 %collective-permute-start.4 = (bf16[8,128,512]{2,0,1:T(8,128)(2,1)}, bf16[8,128,512]{2,0,1:T(8,128)(2,1)S(1)}, u32[]{:S(2)}, u32[]{:S(2)}) collective-permute-start(bf16[8,128,512]{2,0,1:T(8,128)(2,1)} %get-tuple-element.255), channel_id=1, source_target_pairs={{1,0},{4,1},{5,4},{8,5},{9,8},{12,9},{13,12},{3,2},{6,3},{7,6},{10... | collective-permute-start | bytes 3145736 | tf_op jit(solution)/shard_map/ppermute | solution.py:16
  744.7 36.7 %collective-permute-start.5 = (bf16[8,128,512]{2,0,1:T(8,128)(2,1)}, bf16[8,128,512]{2,0,1:T(8,128)(2,1)}, u32[]{:S(2)}, u32[]{:S(2)}) collective-permute-start(bf16[8,128,512]{2,0,1:T(8,128)(2,1)} %get-tuple-element.256), channel_id=1, source_target_pairs={{0,1},{1,4},{4,5},{5,8},{8,9},{9,12},{12,13},{2,3},{3,6},{6,7},{7,... | collective-permute-start | bytes 3145736 | tf_op jit(solution)/shard_map/ppermute | solution.py:16
  752.7 18.5 %all-to-all-start.3 = ((bf16[8,128,512]{2,0,1:T(8,128)(2,1)}), bf16[8,128,512]{2,0,1:T(8,128)(2,1)S(1)}, u32[]{:S(2)}, u32[]{:S(2)}) async-start(bf16[8,128,512]{2,0,1:T(8,128)(2,1)} %copy.164), calls=%async_computation.3 | async-start | bytes 2097152 | tf_op jit(solution)/shard_map/all_to_all | solution.py:107
  762.4 7.1 copy-start.7
  763.8 35.9 %collective-permute-start.6 = (bf16[8,128,512]{2,0,1:T(8,128)(2,1)}, bf16[8,128,512]{2,0,1:T(8,128)(2,1)}, u32[]{:S(2)}, u32[]{:S(2)}) collective-permute-start(bf16[8,128,512]{2,0,1:T(8,128)(2,1)} %get-tuple-element.253), channel_id=1, source_target_pairs={{1,0},{4,1},{5,4},{8,5},{9,8},{12,9},{13,12},{3,2},{6,3},{7,6},{10... | collective-permute-start | bytes 3145736 | tf_op jit(solution)/shard_map/ppermute | solution.py:16
  765.1 34.6 %collective-permute-start.7 = (bf16[8,128,512]{2,0,1:T(8,128)(2,1)}, bf16[8,128,512]{2,0,1:T(8,128)(2,1)}, u32[]{:S(2)}, u32[]{:S(2)}) collective-permute-start(bf16[8,128,512]{2,0,1:T(8,128)(2,1)} %get-tuple-element.254), channel_id=1, source_target_pairs={{0,1},{1,4},{4,5},{5,8},{8,9},{9,12},{12,13},{2,3},{3,6},{6,7},{7,... | collective-permute-start | bytes 3145736 | tf_op jit(solution)/shard_map/ppermute | solution.py:16
  771.1 18.6 %all-to-all-start.5 = ((bf16[8,128,512]{2,0,1:T(8,128)(2,1)}), bf16[8,128,512]{2,0,1:T(8,128)(2,1)S(1)}, u32[]{:S(2)}, u32[]{:S(2)}) async-start(bf16[8,128,512]{2,0,1:T(8,128)(2,1)} %copy.174), calls=%async_computation.5 | async-start | bytes 2097152 | tf_op jit(solution)/shard_map/all_to_all | solution.py:157
  789.7 17.5 %all-to-all-start.6 = ((bf16[8,128,512]{2,0,1:T(8,128)(2,1)}), bf16[8,128,512]{2,0,1:T(8,128)(2,1)S(1)}, u32[]{:S(2)}, u32[]{:S(2)}) async-start(bf16[8,128,512]{2,0,1:T(8,128)(2,1)} %fusion.21), calls=%async_computation.6 | async-start | bytes 2097152 | tf_op jit(solution)/shard_map/all_to_all | solution.py:158
  807.2 17.8 %all-to-all-start.7 = ((bf16[8,128,512]{2,0,1:T(8,128)(2,1)}), bf16[8,128,512]{2,0,1:T(8,128)(2,1)}, u32[]{:S(2)}, u32[]{:S(2)}) async-start(bf16[8,128,512]{2,0,1:T(8,128)(2,1)} %fusion.19), calls=%async_computation.7 | async-start | bytes 2097152 | tf_op jit(solution)/shard_map/all_to_all | solution.py:159
  819.2 9.7 %copy-start.1 = (s32[64,16]{0,1:T(8,128)S(1)}, s32[64,16]{0,1:T(8,128)}, u32[]{:S(2)}) copy-start(s32[64,16]{0,1:T(8,128)} %param.14) | copy-start | bytes 12292
where the time goes:
time: 843 us; the launch traced here: 829 us
  local copies, waits for them, and re-layouts  487 us (58%)
  other arithmetic  179 us (21%)
  matrix products  65.8 us (8%)
  starting transfers between devices  56.7 us (7%)
  waiting for transfers between devices  37.4 us (4%)
    reshape x40, local copies, waits for them, and re-layouts, split_heads(): return tile_rows.reshape(tile_rows.shape[0], tile_rows.shape[1] // DH, DH)  109 us
    scatter-add x8, other arithmetic, own_block(): value_sum.at[slot_block].add(value_part.reshape(-1, BQ, feature_width))  76.4 us
    scatter-add x8, other arithmetic, own_block(): key_sum.at[slot_block].add(key_part.reshape(-1, BQ, feature_width))  76.3 us
    while x64, local copies, waits for them, and re-layouts  63.3 us
    reshape x8, local copies, waits for them, and re-layouts, own_block(): value_part.reshape(-1, BQ, feature_width)  42.3 us
    reshape x8, local copies, waits for them, and re-layouts, own_block(): key_part.reshape(-1, BQ, feature_width)  42.2 us
    dot_general x16, matrix products, scores(): jnp.einsum('qhd,khd->hqk', split_heads(query_block), split_heads(key_bloc...  31.2 us
    gather x8, local copies, waits for them, and re-layouts, forward_block(): value_block = value_wide[slot_block].reshape(-1, feature_width)  31.2 us
  transfers between devices with their start and end apart: 16, of which 6 were waited for; matrix products, arithmetic and copies ran while one was open for 10% of the time, Pallas kernels for 0%

commit v1 on v0

v1 whole, which is shorter than its diff:
```python
import jax
import jax.numpy as jnp
from jax import lax
from jax.experimental import pallas as pl
from jax.experimental.pallas import tpu as pltpu
from jax.sharding import PartitionSpec as P

DH = 128
BQ = 128
NEGATIVE = -1e30
SCALE = DH ** (-0.5)
RING = ("ctx", "sub")


def from_behind(array, by):
    devices = lax.axis_size(RING)
    pairs = [(i, i + by) for i in range(devices) if 0 <= i + by < devices]
    return lax.ppermute(array, RING, pairs)


def lookup(count_table, wanted):
    matches = wanted[..., None] == jnp.arange(count_table.shape[0], dtype=jnp.int32)
    return jnp.sum(jnp.where(matches, count_table, 0), axis=-1)


def mm(a, b, contract):
    return lax.dot_general(a, b, (contract, ((), ())), preferred_element_type=jnp.float32)


def attention_kernel(
    slot_ref, count_ref, valid_ref,
    qg_ref, left_ref, own_ref, right_ref,
    aq_ref, dleft_ref, down_ref, dright_ref,
    rows, cols, sums,
):
    parts, _, blocks, _, _ = own_ref.shape
    block = pl.program_id(1)
    slots = slot_ref.shape[1]

    @pl.when(block == 0)
    def _():
        for which in range(2):
            for side, ref in enumerate((left_ref, own_ref, right_ref)):
                def fill(i, carry, which=which, side=side, ref=ref):
                    tile = ref[:, which, i].reshape(BQ, DH)
                    rows[which, side * blocks + i] = tile
                    cols[which, side * blocks + i] = tile.astype(jnp.float32).T.astype(tile.dtype)
                    return carry
                lax.fori_loop(0, blocks, fill, 0)
        sums[...] = jnp.zeros_like(sums)

    index = [slot_ref[block, s] for s in range(slots)]
    gather = lambda ref, which, axis: jnp.concatenate([ref[which, i] for i in index], axis=axis)
    query = qg_ref[:, 0, 0].reshape(BQ, DH)
    grad = qg_ref[:, 1, 0].reshape(BQ, DH).astype(jnp.float32)
    valid = valid_ref[block]
    grad32 = jnp.where(lax.broadcasted_iota(jnp.int32, (BQ, DH), 0) < valid, grad, 0.0)
    grad_masked = grad32.astype(jnp.bfloat16)

    raw = mm(gather(rows, 0, 0), query, ((1,), (1,)))
    position = lax.broadcasted_iota(jnp.int32, (BQ, BQ), 0)
    logits = jnp.concatenate(
        [
            jnp.where(position < count_ref[block, s], raw[s * BQ : (s + 1) * BQ] * SCALE, NEGATIVE)
            for s in range(slots)
        ],
        axis=0,
    )
    highest = jnp.max(logits, axis=0, keepdims=True)
    weight = jnp.exp(logits - highest)
    probability = weight * (1.0 / jnp.sum(weight, axis=0, keepdims=True))
    prob16 = probability.astype(jnp.bfloat16)
    mixture = mm(gather(cols, 1, 1), prob16, ((1,), (0,)))
    row_ok = lax.broadcasted_iota(jnp.int32, (DH, BQ), 1) < valid
    attended = jnp.where(row_ok, mixture, 0.0).astype(jnp.bfloat16).astype(jnp.float32)
    delta = jnp.sum(attended * grad32.T, axis=0, keepdims=True)
    prob_grad = mm(gather(rows, 1, 0), grad_masked, ((1,), (1,)))
    score_grad = (probability * (prob_grad - delta)).astype(jnp.bfloat16)
    query_grad = mm(gather(cols, 0, 1), score_grad, ((1,), (0,))) * SCALE
    aq_ref[:, 0, 0] = attended.T.astype(jnp.bfloat16).reshape(parts, BQ // parts, DH)
    aq_ref[:, 1, 0] = query_grad.T.astype(jnp.bfloat16).reshape(parts, BQ // parts, DH)
    key_part = mm(score_grad, query, ((1,), (0,)))
    value_part = mm(prob16, grad_masked, ((1,), (0,)))
    for s in range(slots):
        here = slice(s * BQ, (s + 1) * BQ)
        sums[0, index[s]] += key_part[here]
        sums[1, index[s]] += value_part[here]

    @pl.when(block == blocks - 1)
    def _():
        for which in range(2):
            factor = SCALE if which == 0 else 1.0
            for side, ref in enumerate((dleft_ref, down_ref, dright_ref)):
                def drain(i, carry, which=which, side=side, ref=ref, factor=factor):
                    tile = sums[which, side * blocks + i] * factor
                    ref[:, which, i] = tile.astype(ref.dtype).reshape(parts, BQ // parts, DH)
                    return carry
                lax.fori_loop(0, blocks, drain, 0)


def attention(slot, count, valid, qg, left, own, right):
    parts, two, blocks, short, width = own.shape
    heads = width // DH
    one = pl.BlockSpec((parts, two, 1, short, DH), lambda h, b, *_: (0, 0, b, 0, h))
    whole = pl.BlockSpec((parts, two, blocks, short, DH), lambda h, b, *_: (0, 0, 0, 0, h))
    shape = own.shape
    pairs = blocks * heads * slot.shape[1]
    return pl.pallas_call(
        attention_kernel,
        grid_spec=pltpu.PrefetchScalarGridSpec(
            num_scalar_prefetch=3,
            grid=(heads, blocks),
            in_specs=[one, whole, whole, whole],
            out_specs=[one, whole, whole, whole],
            scratch_shapes=[
                pltpu.VMEM((2, 3 * blocks, BQ, DH), jnp.bfloat16),
                pltpu.VMEM((2, 3 * blocks, DH, BQ), jnp.bfloat16),
                pltpu.VMEM((2, 3 * blocks, BQ, DH), jnp.float32),
            ],
        ),
        out_shape=[
            jax.ShapeDtypeStruct(shape, jnp.bfloat16),
            jax.ShapeDtypeStruct(shape, jnp.bfloat16),
            jax.ShapeDtypeStruct(shape, jnp.float32),
            jax.ShapeDtypeStruct(shape, jnp.bfloat16),
        ],
        compiler_params=pltpu.CompilerParams(
            dimension_semantics=("arbitrary", "arbitrary"), vmem_limit_bytes=48 * 1024 * 1024
        ),
        cost_estimate=pl.CostEstimate(
            flops=12 * pairs * BQ * BQ * DH,
            bytes_accessed=12 * own.size * 2,
            transcendentals=pairs * BQ * BQ,
        ),
    )(slot, count, valid, qg, left, own, right)


def to_heads(first, second):
    parts = lax.axis_size("head")
    pair = jnp.stack([first, second])
    two, blocks, short, features = pair.shape
    pair = pair.reshape(two, blocks, short, parts, features // parts).transpose(3, 0, 1, 2, 4)
    return lax.all_to_all(pair, "head", split_axis=0, concat_axis=0, tiled=True)


def to_points(pair):
    pair = lax.all_to_all(pair, "head", split_axis=0, concat_axis=0, tiled=True)
    parts, two, blocks, short, width = pair.shape
    pair = pair.transpose(1, 2, 3, 0, 4).reshape(two, blocks, short, parts * width)
    return pair[0], pair[1]


def shards(query_rows, key_rows, value_rows, cotangent, neighbours, valid_counts):
    blocks = query_rows.shape[0]
    own = to_heads(key_rows, value_rows)
    left = from_behind(own, 1)
    right = from_behind(own, -1)
    qg = to_heads(query_rows, cotangent)
    first_block = lax.axis_index(RING) * blocks
    own_lists = lax.dynamic_slice_in_dim(neighbours, first_block, blocks, 0)
    own_counts = lax.dynamic_slice_in_dim(valid_counts, first_block, blocks, 0)
    slot = jnp.clip(own_lists - (first_block - blocks), 0, 3 * blocks - 1)
    count = jnp.where(own_lists >= 0, lookup(valid_counts, own_lists), 0)
    aq, dleft, down, dright = attention(slot, count, own_counts, qg, left, own, right)
    from_right = from_behind(dleft, -1).astype(jnp.float32)
    from_left = from_behind(dright, 1).astype(jnp.float32)
    attended, query_grad = to_points(aq)
    total = (down + from_right + from_left).astype(jnp.bfloat16)
    key_grad, value_grad = to_points(total)
    return (attended, query_grad, key_grad, value_grad)


def solution(mesh):
    placed = P(("groups", "ctx", "sub"), "head", None)
    return jax.shard_map(
        shards,
        mesh=mesh,
        in_specs=(placed,) * 4 + (P("groups", None), P("groups")),
        out_specs=(placed,) * 4,
        check_vma=False,
    )
```

time: 843 us -> 235 us (0.28); the launches traced: 829 us -> 234 us
  local copies, waits for them, and re-layouts: 487 us -> 21.3 us
  other arithmetic: 179 us -> 7.87 us
  Pallas kernels: 0 us -> 91.4 us
  matrix products: 65.8 us -> 0 us
  starting transfers between devices: 56.7 us -> 24.2 us
  blocking collectives: 0 us -> 29.8 us
  waiting for transfers between devices: 37.4 us -> 58.5 us
    reshape x56 -> x0, local copies, waits for them, and re-layouts: 194 us -> none  [the longest x40 109 us: split_heads(): return tile_rows.reshape(tile_rows.shape[0], tile_rows.shape[1] // DH, DH)]
    scatter-add x16 -> x0, other arithmetic: 153 us -> none  [the longest x8 76.4 us: own_block(): value_sum.at[slot_block].add(value_part.reshape(-1, BQ, feature_width))]
    gather x32 -> x0, local copies, waits for them, and re-layouts: 103 us -> none  [the longest x8 31.2 us: forward_block(): value_block = value_wide[slot_block].reshape(-1, feature_width)]
    while x71 -> x0, local copies, waits for them, and re-layouts: 93.1 us -> none
    pallas_call x0 -> x1, Pallas kernels: none -> 91.4 us  [attention(): pl.pallas_call(attention_kernel, grid_spec=pltpu.PrefetchScalarGridSpec(n...]
    dot_general x56 -> x0, matrix products: 65.8 us -> none  [the longest x16 31.2 us: scores(): jnp.einsum('qhd,khd->hqk', split_heads(query_block), split_heads(key_bloc...]
    all_to_all x0 -> x1, blocking collectives: none -> 29.8 us  [to_heads(): return lax.all_to_all(pair, 'head', split_axis=0, concat_axis=0, tiled=True)]
    unnamed x26 -> x13, local copies, waits for them, and re-layouts: 30.5 us -> 1.39 us
  transfers between devices with their start and end apart: 16 -> 7, of which waited for: 6 -> 3; matrix products, arithmetic and copies ran while one was open for 10% -> 8% of each run, Pallas kernels for 0% -> 0%
where the time goes in v1:
time: 235 us; the launch traced here: 234 us
  Pallas kernels  91.4 us (39%)
  waiting for transfers between devices  58.5 us (25%)
  blocking collectives  29.8 us (13%)
  starting transfers between devices  24.2 us (10%)
  local copies, waits for them, and re-layouts  21.3 us (9%)
  other arithmetic  7.87 us (3%)
    pallas_call x1, Pallas kernels, attention(): pl.pallas_call(attention_kernel, grid_spec=pltpu.PrefetchScalarGridSpec(n...  91.4 us
    all_to_all x2, waiting for transfers between devices, to_points(): pair = lax.all_to_all(pair, 'head', split_axis=0, concat_axis=0, tiled=True)  33.6 us
    all_to_all x1, blocking collectives, to_heads(): return lax.all_to_all(pair, 'head', split_axis=0, concat_axis=0, tiled=True)  29.8 us
    all_to_all x1, waiting for transfers between devices, to_heads(): return lax.all_to_all(pair, 'head', split_axis=0, concat_axis=0, tiled=True)  24.9 us
    ppermute x4, starting transfers between devices, from_behind(): return lax.ppermute(array, RING, pairs)  11.4 us
    all_to_all x2, starting transfers between devices, to_points(): pair = lax.all_to_all(pair, 'head', split_axis=0, concat_axis=0, tiled=True)  8.83 us
    slice x6, local copies, waits for them, and re-layouts, to_points(): return (pair[0], pair[1])  8.51 us
    squeeze x4, local copies, waits for them, and re-layouts, to_points(): return (pair[0], pair[1])  6.19 us
  transfers between devices with their start and end apart: 7, of which 3 were waited for; matrix products, arithmetic and copies ran while one was open for 8% of the time, Pallas kernels for 0%

profile of v1, /device:TPU:0, one launch (start us, length us, event | category | flops | bytes accessed | tf_op | source)
XLA Modules:
  0.0 234.0 jit_solution(10139328340549361120)
XLA Ops:
  0.6 0.0 copy-start
  0.6 0.0 copy-start.2
  0.7 1.9 stack.21
  2.6 0.2 copy.23
  2.8 0.0 copy-done.2
  2.8 0.8 stack.22
  3.6 0.2 copy.24
  3.8 0.2 maximum_bitcast_fusion.1
  4.0 0.0 copy-start.3
  4.0 29.8 %all_to_all.20.own_ref = bf16[2,2,8,64,512]{4,3,2,1,0:T(8,128)(2,1)} all-to-all(bf16[2,2,8,64,512]{4,3,2,1,0:T(8,128)(2,1)S(1)} %maximum_bitcast_fusion.1), channel_id=1, replica_groups=mesh['groups'=2,'ctx'=4,'head'=2,'sub'=2] {'head'}, dimensions={0} | all-to-all | bytes 4194304 | tf_op jit(solution)/shard_map/all_to_all | solution.py:143
  33.9 1.4 collective-permute-start.1
  35.3 4.4 %collective-permute-start = (bf16[2,2,8,64,512]{4,3,2,1,0:T(8,128)(2,1)}, bf16[2,2,8,64,512]{4,3,2,1,0:T(8,128)(2,1)}, u32[]{:S(2)}, u32[]{:S(2)}) collective-permute-start(bf16[2,2,8,64,512]{4,3,2,1,0:T(8,128)(2,1)} %all_to_all.20.own_ref), channel_id=1, source_target_pairs={{0,1},{1,4},{4,5},{5,8},{8,9},{9,12},{12,13},{2,3},{3,6},{6,7},{7,... | collective-permute-start | bytes 6291464 | tf_op jit(solution)/shard_map/ppermute | solution.py:18
  39.7 0.0 copy-done.3
  39.7 0.8 stack.18
  40.5 0.2 copy.21
  40.7 0.0 copy-done.4
  40.7 0.8 stack.19
  41.5 0.2 copy.22
  41.7 1.5 maximum_bitcast_fusion
  43.2 3.9 %all-to-all-start = ((bf16[2,2,8,64,512]{4,3,2,1,0:T(8,128)(2,1)}), bf16[2,2,8,64,512]{4,3,2,1,0:T(8,128)(2,1)S(1)}, u32[]{:S(2)}, u32[]{:S(2)}) async-start(bf16[2,2,8,64,512]{4,3,2,1,0:T(8,128)(2,1)} %maximum_bitcast_fusion), calls=%async_computation | async-start | bytes 4194304 | tf_op jit(solution)/shard_map/all_to_all | solution.py:143
  47.1 0.1 dynamic_slice.7.valid_ref
  47.2 0.1 constant_dynamic-slice_fusion
  47.3 0.1 copy.29
  47.4 0.3 select_reduce_fusion
  47.7 24.9 %all-to-all-done.qg_ref = bf16[2,2,8,64,512]{4,3,2,1,0:T(8,128)(2,1)S(1)} async-done(((bf16[2,2,8,64,512]{4,3,2,1,0:T(8,128)(2,1)}), bf16[2,2,8,64,512]{4,3,2,1,0:T(8,128)(2,1)S(1)}, u32[]{:S(2)}, u32[]{:S(2)}) %all-to-all-start) | async-done | bytes 2097184 | tf_op jit(solution)/shard_map/all_to_all | solution.py:143
  72.6 0.0 collective-permute-done.1.right_ref
  72.6 0.0 collective-permute-done.left_ref
  72.6 1.3 copy-done.1
  73.9 91.4 %shard_map.93 = (bf16[2,2,8,64,512]{4,3,2,1,0:T(8,128)(2,1)}, bf16[2,2,8,64,512]{4,3,2,1,0:T(8,128)(2,1)S(1)}, f32[2,2,8,64,512]{4,3,2,1,0:T(8,128)}, bf16[2,2,8,64,512]{4,3,2,1,0:T(8,128)(2,1)}) custom-call(s32[8,16]{1,0:T(8,128)S(1)} %get-tuple-element.17.slot_ref, s32[8,16]{1,0:T(8,128)S(1)} %get-tuple-element.16.count_ref, s32[8]{0:T(128)S(1)} %dynamic_slice.7.valid_ref, ...), custom_call_target="tpu_custom_call" | custom-call | flops 12884901888 | bytes 25165824 | tf_op jit(solution)/shard_map/pallas_call | solution.py:108
  165.3 1.3 collective-permute-start.2
  166.6 4.4 %collective-permute-start.3 = (bf16[2,2,8,64,512]{4,3,2,1,0:T(8,128)(2,1)}, bf16[2,2,8,64,512]{4,3,2,1,0:T(8,128)(2,1)}, u32[]{:S(2)}, u32[]{:S(2)}) collective-permute-start(bf16[2,2,8,64,512]{4,3,2,1,0:T(8,128)(2,1)} %get-tuple-element.11), channel_id=1, source_target_pairs={{0,1},{1,4},{4,5},{5,8},{8,9},{9,12},{12,13},{2,3},{3,6},{6,7},{7,... | collective-permute-start | bytes 6291464 | tf_op jit(solution)/shard_map/ppermute | solution.py:18
  170.9 4.9 %all-to-all-start.2 = ((bf16[2,2,8,64,512]{4,3,2,1,0:T(8,128)(2,1)}), bf16[2,2,8,64,512]{4,3,2,1,0:T(8,128)(2,1)}, u32[]{:S(2)}, u32[]{:S(2)}) async-start(bf16[2,2,8,64,512]{4,3,2,1,0:T(8,128)(2,1)} %get-tuple-element.8), calls=%async_computation.2 | async-start | bytes 4194304 | tf_op jit(solution)/shard_map/all_to_all | solution.py:147
  175.8 0.0 collective-permute-done.2
  175.9 0.0 collective-permute-done.3
  175.9 5.8 %add_convert_fusion = bf16[2,2,8,64,512]{4,3,2,1,0:T(8,128)(2,1)} fusion(bf16[2,2,8,64,512]{4,3,2,1,0:T(8,128)(2,1)} %collective-permute-done.3, f32[2,2,8,64,512]{4,3,2,1,0:T(8,128)} %get-tuple-element.9, bf16[2,2,8,64,512]{4,3,2,1,0:T(8,128)(2,1)} %collective-permute-done.2), kind=kLoop, calls=%fused_computation | loop fusion | flops 5242880 | bytes 10485760 | tf_op jit(solution)/shard_map/convert_element_type | solution.py:168
  181.7 18.9 %all-to-all-done.2 = bf16[2,2,8,64,512]{4,3,2,1,0:T(8,128)(2,1)} async-done(((bf16[2,2,8,64,512]{4,3,2,1,0:T(8,128)(2,1)}), bf16[2,2,8,64,512]{4,3,2,1,0:T(8,128)(2,1)}, u32[]{:S(2)}, u32[]{:S(2)}) %all-to-all-start.2) | async-done | bytes 2097184 | tf_op jit(solution)/shard_map/all_to_all | solution.py:147
  200.6 3.9 %all-to-all-start.3 = ((bf16[2,2,8,64,512]{4,3,2,1,0:T(8,128)(2,1)}), bf16[2,2,8,64,512]{4,3,2,1,0:T(8,128)(2,1)S(1)}, u32[]{:S(2)}, u32[]{:S(2)}) async-start(bf16[2,2,8,64,512]{4,3,2,1,0:T(8,128)(2,1)} %add_convert_fusion), calls=%async_computation.3 | async-start | bytes 4194304 | tf_op jit(solution)/shard_map/all_to_all | solution.py:147
  204.6 2.7 %fusion.1 = (bf16[1,8,64,2,512]{4,2,1,0,3:T(8,128)(2,1)S(1)}, bf16[1,8,64,2,512]{4,2,1,0,3:T(8,128)(2,1)}) fusion(bf16[2,8,64,2,512]{4,2,1,0,3:T(8,128)(2,1)} %bitcast.2), kind=kLoop, calls=%fused_computation.9 | loop fusion | bytes 4194304 | tf_op jit(solution)/shard_map/slice | solution.py:150
  207.3 1.1 copy.26
  208.4 1.5 squeeze.13
  210.0 2.3 copy.25
  212.3 1.5 squeeze.12
  213.8 14.7 %all-to-all-done.3 = bf16[2,2,8,64,512]{4,3,2,1,0:T(8,128)(2,1)S(1)} async-done(((bf16[2,2,8,64,512]{4,3,2,1,0:T(8,128)(2,1)}), bf16[2,2,8,64,512]{4,3,2,1,0:T(8,128)(2,1)S(1)}, u32[]{:S(2)}, u32[]{:S(2)}) %all-to-all-start.3) | async-done | bytes 2097184 | tf_op jit(solution)/shard_map/all_to_all | solution.py:147
  228.5 0.2 fusion
  228.7 1.1 copy.28
  229.8 1.5 squeeze.15
  231.4 1.1 copy.27
  232.5 1.5 squeeze.14
  (6 shorter events, 0.0 us)
Async XLA Ops:
  0.6 46.6 %copy-start = (s32[64,16]{0,1:T(8,128)S(1)}, s32[64,16]{0,1:T(8,128)}, u32[]{:S(2)}) copy-start(s32[64,16]{0,1:T(8,128)} %param.10) | copy-start | bytes 12292
  0.6 2.2 copy-start.2
  4.0 35.7 %copy-start.3 = (bf16[8,64,1024]{2,1,0:T(8,128)(2,1)S(1)}, bf16[8,64,1024]{2,1,0:T(8,128)(2,1)}, u32[]{:S(2)}) copy-start(bf16[8,64,1024]{2,1,0:T(8,128)(2,1)} %param.6) | copy-start | bytes 3145732
  33.9 6.8 %copy-start.4 = (bf16[8,64,1024]{2,1,0:T(8,128)(2,1)S(1)}, bf16[8,64,1024]{2,1,0:T(8,128)(2,1)}, u32[]{:S(2)}) copy-start(bf16[8,64,1024]{2,1,0:T(8,128)(2,1)} %param.9) | copy-start | bytes 3145732
  33.9 38.7 %collective-permute-start.1 = (bf16[2,2,8,64,512]{4,3,2,1,0:T(8,128)(2,1)}, bf16[2,2,8,64,512]{4,3,2,1,0:T(8,128)(2,1)}, u32[]{:S(2)}, u32[]{:S(2)}) collective-permute-start(bf16[2,2,8,64,512]{4,3,2,1,0:T(8,128)(2,1)} %all_to_all.20.own_ref), channel_id=1, source_target_pairs={{1,0},{4,1},{5,4},{8,5},{9,8},{12,9},{13,12},{3,2},{6,3},{7,6},{10... | collective-permute-start | bytes 6291464 | tf_op jit(solution)/shard_map/ppermute | solution.py:18
  35.3 37.3 %collective-permute-start = (bf16[2,2,8,64,512]{4,3,2,1,0:T(8,128)(2,1)}, bf16[2,2,8,64,512]{4,3,2,1,0:T(8,128)(2,1)}, u32[]{:S(2)}, u32[]{:S(2)}) collective-permute-start(bf16[2,2,8,64,512]{4,3,2,1,0:T(8,128)(2,1)} %all_to_all.20.own_ref), channel_id=1, source_target_pairs={{0,1},{1,4},{4,5},{5,8},{8,9},{9,12},{12,13},{2,3},{3,6},{6,7},{7,... | collective-permute-start | bytes 6291464 | tf_op jit(solution)/shard_map/ppermute | solution.py:18
  43.2 3.9 %copy-start.5 = (s32[64]{0:T(128)S(1)}, s32[64]{0:T(128)}, u32[]{:S(2)}) copy-start(s32[64]{0:T(128)} %param.11) | copy-start | bytes 772
  43.2 29.4 %all-to-all-start = ((bf16[2,2,8,64,512]{4,3,2,1,0:T(8,128)(2,1)}), bf16[2,2,8,64,512]{4,3,2,1,0:T(8,128)(2,1)S(1)}, u32[]{:S(2)}, u32[]{:S(2)}) async-start(bf16[2,2,8,64,512]{4,3,2,1,0:T(8,128)(2,1)} %maximum_bitcast_fusion), calls=%async_computation | async-start | bytes 4194304 | tf_op jit(solution)/shard_map/all_to_all | solution.py:143
  72.6 1.3 copy-start.1
  165.3 10.6 %collective-permute-start.2 = (bf16[2,2,8,64,512]{4,3,2,1,0:T(8,128)(2,1)S(1)}, bf16[2,2,8,64,512]{4,3,2,1,0:T(8,128)(2,1)}, u32[]{:S(2)}, u32[]{:S(2)}) collective-permute-start(bf16[2,2,8,64,512]{4,3,2,1,0:T(8,128)(2,1)S(1)} %get-tuple-element.10), channel_id=1, source_target_pairs={{1,0},{4,1},{5,4},{8,5},{9,8},{12,9},{13,12},{3,2},{6,3},{7,6},{10... | collective-permute-start | bytes 6291464 | tf_op jit(solution)/shard_map/ppermute | solution.py:18
  166.6 9.3 %collective-permute-start.3 = (bf16[2,2,8,64,512]{4,3,2,1,0:T(8,128)(2,1)}, bf16[2,2,8,64,512]{4,3,2,1,0:T(8,128)(2,1)}, u32[]{:S(2)}, u32[]{:S(2)}) collective-permute-start(bf16[2,2,8,64,512]{4,3,2,1,0:T(8,128)(2,1)} %get-tuple-element.11), channel_id=1, source_target_pairs={{0,1},{1,4},{4,5},{5,8},{8,9},{9,12},{12,13},{2,3},{3,6},{6,7},{7,... | collective-permute-start | bytes 6291464 | tf_op jit(solution)/shard_map/ppermute | solution.py:18
  170.9 29.7 %all-to-all-start.2 = ((bf16[2,2,8,64,512]{4,3,2,1,0:T(8,128)(2,1)}), bf16[2,2,8,64,512]{4,3,2,1,0:T(8,128)(2,1)}, u32[]{:S(2)}, u32[]{:S(2)}) async-start(bf16[2,2,8,64,512]{4,3,2,1,0:T(8,128)(2,1)} %get-tuple-element.8), calls=%async_computation.2 | async-start | bytes 4194304 | tf_op jit(solution)/shard_map/all_to_all | solution.py:147
  200.6 27.9 %all-to-all-start.3 = ((bf16[2,2,8,64,512]{4,3,2,1,0:T(8,128)(2,1)}), bf16[2,2,8,64,512]{4,3,2,1,0:T(8,128)(2,1)S(1)}, u32[]{:S(2)}, u32[]{:S(2)}) async-start(bf16[2,2,8,64,512]{4,3,2,1,0:T(8,128)(2,1)} %add_convert_fusion), calls=%async_computation.3 | async-start | bytes 4194304 | tf_op jit(solution)/shard_map/all_to_all | solution.py:147
